TPU v7x, 128 devices: a whole 4x4x4 slice. The times are simulated.
128 devices in a mesh: row: 16 (over z, y_hi, core), col: 8 (over x, y_lo).
Axes of the slice: x: 4, y: 4 (y_hi: 2, y_lo: 2; y = y_hi * 2 + y_lo), z: 4, core: 2. Of those that a mesh axis runs over, the one named last changes fastest.
Arguments:
- roll_hidden: bfloat16 [5376, 4096], P(('row', 'col')), may hold values from -6 to 6
- roll_cotangent: bfloat16 [5376, 4096], P(('row', 'col')), may hold values from -6 to 6
- lengths: int32 [128], P(('row', 'col')), may hold values from 1 to 42, as said below
- owners: int32 [128], P(('row', 'col')), may hold values from 0 to 15, as said below
- prompts: int32 [128], P(('row', 'col')), may hold values from 0 to 15
- rewards: float32 [128], P(('row', 'col')), may hold values from -5 to 5
- gate_weight: bfloat16 [4096, 14784], P('col', 'row'), may hold values from -0.09375 to 0.09375
- up_weight: bfloat16 [4096, 14784], P('col', 'row'), may hold values from -0.09375 to 0.09375
- down_weight: bfloat16 [14784, 4096], P('row', 'col'), may hold values from -0.046875 to 0.046875
Outputs:
- grad_input: bfloat16 [2048, 4096], P('row', 'col')
- grad_gate: bfloat16 [4096, 14784], P('col', 'row')
- grad_up: bfloat16 [4096, 14784], P('col', 'row')
- grad_down: bfloat16 [14784, 4096], P('row', 'col')
Inputs may be any that keep to these rules, and one draw needn't show every extreme that they name: `owners`: each owner value names exactly 8 rows; the lengths of one owner's rows sum to at most 128, and to exactly 128 for some owner in every draw. `lengths`: some row has length 42 in every draw.
All inputs are finite; a program needn't handle non-finite values.
Results may differ from a plain program's by a relative error of at most 0.025.
Values may be sent and summed in bfloat16 or wider, within the bound.
No kernel may reach another device: no remote copies, remote signals or barrier semaphores. Data moves between devices by JAX's collectives and lax.ppermute only.
A program may use at most 128 MiB of HBM per device.

v0:
```python
import jax
import jax.numpy as jnp
from jax import lax
from jax.sharding import PartitionSpec as P

CAPR = 128
spread_floor = 0.7


def in_one_piece(arrays, axis, split_dim, concat_dim, along):
    ends, at = ([], 0)
    for a in arrays[:-1]:
        at += a.shape[along]
        ends.append(at)
    both = jnp.concatenate(arrays, axis=along)
    return tuple(
        jnp.split(
            lax.all_to_all(both, axis, split_axis=split_dim, concat_axis=concat_dim, tiled=True),
            ends,
            axis=along,
        )
    )


def sent_together(arrays, axis, dim, along):
    widths = [a.shape[along] for a in arrays]
    both = jnp.concatenate(arrays, axis=along)
    result = lax.all_gather(both, axis, axis=dim, tiled=True)
    return tuple(jnp.split(result, [sum(widths[:k]) for k in range(1, len(widths))], axis=along))


def cut_along(array, dim, size):
    lengths = array.shape
    tiles = array.reshape(*lengths[:dim], size, lengths[dim] // size, *lengths[dim + 1 :])
    return jnp.moveaxis(tiles, dim, 0)


def sent_and_summed(array, axis, dim):
    size = lax.axis_size(axis)
    tiles = lax.all_to_all(cut_along(array, dim, size), axis, 0, 0, tiled=True)
    return jnp.sum(tiles.astype(jnp.float32), axis=0)


def row_weights(lengths, prompts, rewards, count_prompts):
    onehot = (prompts[:, None] == jnp.arange(count_prompts, dtype=jnp.int32)[None, :]).astype(
        jnp.float32
    )
    counts = jnp.maximum(jnp.sum(onehot, 0), 1.0)
    means = jnp.sum(onehot * rewards[:, None], 0) / counts
    centred = rewards - jnp.sum(onehot * means[None, :], 1)
    spreads = jnp.sqrt(jnp.sum(onehot * (centred * centred)[:, None], 0) / counts)
    divisor = jnp.maximum(jnp.sum(onehot * spreads[None, :], 1), spread_floor)
    return centred / divisor / lengths.astype(jnp.float32)


def row_offsets(lengths, owners):
    count = lengths.shape[0]
    places = jnp.arange(count, dtype=jnp.int32)
    earlier = (owners[None, :] == owners[:, None]) & (places[None, :] < places[:, None])
    return jnp.sum(jnp.where(earlier, lengths[None, :], 0), 1)


def source_index(lengths, owners, offsets, slot_count, capacity, total):
    count = lengths.shape[0]
    slots = jnp.arange(slot_count, dtype=jnp.int32)
    live = slots[None, :] < lengths[:, None]
    target = jnp.where(live, owners[:, None] * capacity + offsets[:, None] + slots[None, :], total)
    flat_source = slots[None, :] * count + jnp.arange(count, dtype=jnp.int32)[:, None]
    empty = jnp.full((total,), slot_count * count, jnp.int32)
    return empty.at[target.reshape(-1)].set(flat_source.reshape(-1), mode="drop")


def per_device(
    roll_hidden,
    roll_cotangent,
    lengths,
    owners,
    prompts,
    rewards,
    gate_weight,
    up_weight,
    down_weight,
):
    row_count = lax.axis_size("row")
    col_count = lax.axis_size("col")
    total_tokens = row_count * CAPR
    count_prompts = row_count * col_count // 8
    slot_count = roll_hidden.shape[0]
    width = roll_hidden.shape[1] // col_count
    local = jnp.stack(
        [
            lengths.astype(jnp.float32),
            owners.astype(jnp.float32),
            prompts.astype(jnp.float32),
            rewards,
        ],
        axis=1,
    )
    table = lax.all_gather(local, ("row", "col"), axis=0, tiled=True)
    all_lengths = table[:, 0].astype(jnp.int32)
    all_owners = table[:, 1].astype(jnp.int32)
    all_prompts = table[:, 2].astype(jnp.int32)
    weights = row_weights(all_lengths, all_prompts, table[:, 3], count_prompts)
    offsets = row_offsets(all_lengths, all_owners)
    mine = lax.dynamic_slice_in_dim(weights, lax.axis_index(("row", "col")), 1, 0)
    live = (jnp.arange(slot_count, dtype=jnp.int32) < lengths[0])[:, None]
    upstream = jnp.where(live, roll_cotangent.astype(jnp.float32) * mine[0], 0.0).astype(
        jnp.bfloat16
    )
    hidden_blocks = roll_hidden.reshape(slot_count, col_count, width)
    upstream_blocks = upstream.reshape(slot_count, col_count, width)
    hidden_cols, upstream_cols = in_one_piece((hidden_blocks, upstream_blocks), "col", 1, 1, 0)
    hidden_all, upstream_all = sent_together((hidden_cols, upstream_cols), "row", 1, 0)
    sources = source_index(all_lengths, all_owners, offsets, slot_count, CAPR, total_tokens)
    packed = jnp.take(hidden_all.reshape(-1, width), sources, axis=0, mode="fill", fill_value=0)
    packed_grad = jnp.take(
        upstream_all.reshape(-1, width), sources, axis=0, mode="fill", fill_value=0
    )
    gate_term = jnp.dot(packed, gate_weight, preferred_element_type=jnp.float32)
    up_term = jnp.dot(packed, up_weight, preferred_element_type=jnp.float32)
    gate, upval = (
        lax.psum(gate_term.astype(jnp.bfloat16), "col").astype(jnp.float32),
        lax.psum(up_term.astype(jnp.bfloat16), "col").astype(jnp.float32),
    )
    sig = jax.nn.sigmoid(gate)
    silu = gate * sig
    hidden = (silu * upval).astype(jnp.bfloat16)
    contract_cols = (((1,), (1,)), ((), ()))
    grad_term = lax.dot_general(
        packed_grad, down_weight, contract_cols, preferred_element_type=jnp.float32
    )
    grad_hidden = lax.psum(grad_term.astype(jnp.bfloat16), "col").astype(jnp.float32)
    grad_gate_act = (grad_hidden * upval * sig * (1.0 + gate * (1.0 - sig))).astype(jnp.bfloat16)
    grad_up_act = (grad_hidden * silu).astype(jnp.bfloat16)
    contract_rows = (((0,), (0,)), ((), ()))
    grad_down = lax.dot_general(
        hidden, packed_grad, contract_rows, preferred_element_type=jnp.float32
    ).astype(jnp.bfloat16)
    grad_gate = lax.dot_general(
        packed, grad_gate_act, contract_rows, preferred_element_type=jnp.float32
    ).astype(jnp.bfloat16)
    grad_up = lax.dot_general(
        packed, grad_up_act, contract_rows, preferred_element_type=jnp.float32
    ).astype(jnp.bfloat16)
    term = lax.dot_general(
        grad_gate_act, gate_weight, contract_cols, preferred_element_type=jnp.float32
    )
    grad_input = sent_and_summed(
        (
            term
            + lax.dot_general(
                grad_up_act, up_weight, contract_cols, preferred_element_type=jnp.float32
            )
        ).astype(jnp.bfloat16),
        "row",
        0,
    )
    return (grad_input.astype(jnp.bfloat16), grad_gate, grad_up, grad_down)


def solution(mesh):
    return jax.shard_map(
        per_device,
        mesh=mesh,
        in_specs=(
            P(("row", "col"), None),
            P(("row", "col"), None),
            P(("row", "col")),
            P(("row", "col")),
            P(("row", "col")),
            P(("row", "col")),
            P("col", "row"),
            P("col", "row"),
            P("row", "col"),
        ),
        out_specs=(P("row", "col"), P("col", "row"), P("col", "row"), P("row", "col")),
        check_vma=False,
    )
```

profile of v0, /device:TPU:4, one launch (start us, length us, event | category | flops | bytes accessed | tf_op | source)
XLA Modules:
  0.0 991.0 jit_solution(10023484400698001869)
XLA Ops:
  7.2 0.0 copy-start
  7.2 0.0 all-gather.3.cloned.1.call-start
  9.9 0.1 maximum_bitcast_fusion
  10.0 307.3 %all-gather = f32[128,1,4]{2,1,0:T(1,128)S(1)} all-gather(f32[1,1,4]{2,1,0:T(1,128)S(1)} %maximum_bitcast_fusion), channel_id=1, replica_groups=mesh['row'=16,'col'=8] {'row','col'}, dimensions={0}, use_global_device_ids=true | all-gather | bytes 2064 | tf_op jit(solution)/shard_map/all_gather | solution.py:99
  317.3 0.1 copy.27
  317.3 0.1 convert_reduce_fusion
  317.5 0.1 select_reduce_fusion.3
  317.6 0.1 select_reduce_fusion.2
  317.7 0.1 select_reduce_fusion.1
  317.8 0.6 dynamic_slice.3
  318.4 1.8 select_convert_fusion
  320.2 0.1 copy.31
  320.3 1.1 copy.30
  321.5 0.1 pad_maximum_fusion
  321.6 0.2 copy.28
  321.8 19.5 %all_to_all.10 = bf16[84,8,512]{2,0,1:T(8,128)(2,1)S(1)} all-to-all(bf16[84,8,512]{2,0,1:T(8,128)(2,1)S(1)} %copy.28), channel_id=1, replica_groups=mesh['row'=16,'col'=8] {'col'}, dimensions={1} | all-to-all | bytes 1376256 | tf_op jit(solution)/shard_map/all_to_all | solution.py:18
  341.3 1.1 copy.29
  342.3 0.0 all-gather.3.cloned.1.call-update
  342.4 0.0 all-reduce.3.cloned.1.call-start
  342.4 0.1 reshape.149
  342.6 0.2 select_reduce_fusion
  342.8 0.1 add_select_fusion
  342.9 0.2 select_n.47
  343.0 0.1 fusion.15
  343.1 20.4 %scatter_custom_fusion = s32[2048]{0:T(1024)S(1)} fusion(s32[5376]{0:T(1024)S(1)} %fusion.15, s32[5376]{0:T(1024)S(1)} %reshape.149, s32[]{:T(128)} %constant.19.clone.1), kind=kCustom, calls=%fused_computation.47 | custom fusion | bytes 8196 | tf_op jit(solution)/shard_map/scatter | solution.py:70
  363.5 65.8 %all-gather.3.cloned.1.call-done = bf16[84,128,512]{2,1,0:T(8,128)(2,1)} async-done(((bf16[84,8,512]{2,1,0:T(8,128)(2,1)}), bf16[84,128,512]{2,1,0:T(8,128)(2,1)}) %all-gather.3.cloned.1.call-update) | async-done | bytes 11010064 | tf_op jit(solution)/shard_map/all_gather | solution.py:28
  429.3 9.6 fusion.25
  438.9 10.9 %gather_fusion = bf16[2048,512]{1,0:T(8,128)(2,1)S(1)} fusion(bf16[5376,512]{1,0:T(8,128)(2,1)} %bitcast.57, s32[2048]{0:T(1024)S(1)} %fusion.16), kind=kCustom, calls=%fused_computation.clone | custom fusion | bytes 4202496 | tf_op jit(solution)/shard_map/jit(_take)/gather | solution.py:116
  449.8 0.0 copy-start.5
  449.8 13.2 %gather_fusion.1 = bf16[2048,512]{1,0:T(8,128)(2,1)} fusion(bf16[5376,512]{1,0:T(8,128)(2,1)} %bitcast.56, s32[2048]{0:T(1024)S(1)} %fusion.16), kind=kCustom, calls=%fused_computation.1.clone | custom fusion | bytes 4202496 | tf_op jit(solution)/shard_map/jit(_take)/gather | solution.py:115
  463.0 0.0 copy-done
  463.0 0.0 copy-start.7
  463.0 0.0 copy-start.10
  463.0 5.9 convolution_convert_fusion
  468.9 0.0 copy-done.7
  468.9 0.0 copy-done.10
  468.9 0.0 copy-start.9
  468.9 3.9 convolution_convert_fusion.1
  472.8 0.0 copy-done.5
  472.8 0.0 copy-done.9
  472.8 3.9 convolution_convert_fusion.2
  476.6 0.0 all-reduce.3.cloned.1.call-update
  476.7 455.9 %all-reduce.3.cloned.1.call-done = (bf16[2048,924]{0,1:T(8,128)(2,1)}, bf16[2048,924]{0,1:T(8,128)(2,1)}, bf16[2048,924]{0,1:T(8,128)(2,1)}) async-done(((bf16[2048,924]{0,1:T(8,128)(2,1)}, bf16[2048,924]{0,1:T(8,128)(2,1)}, bf16[2048,924]{0,1:T(8,128)(2,1)}), (bf16[2048,924]{0,1:T(8,128)(2,1)}, bf16[2048,924]{0,1:T(8,128)(2,1)}, bf16[2048,924]{0,1:T(8,128)(2,1)})) %all-reduce.3.cloned.1.call-update) | async-done | bytes 11354128 | tf_op jit(solution)/shard_map/psum | solution.py:123
  932.6 7.3 fusion
  939.9 0.0 copy-start.4
  939.9 0.0 copy-done.8
  939.9 3.1 convolution_convert_fusion.3
  943.0 0.0 copy-done.4
  943.0 2.4 fusion.26
  945.5 0.0 copy-done.11
  945.5 3.9 add_convert_fusion
  949.4 4.5 all-to-all-start.1
  953.9 0.0 copy-start.2
  953.9 0.0 copy-start.3
  953.9 0.0 copy-start.6
  953.9 6.0 convolution_convert_fusion.4
  959.9 0.0 copy-done.2
  959.9 0.0 copy-done.3
  959.9 0.0 copy-done.6
  959.9 0.0 copy-start.1
  959.9 3.5 fusion.11
  963.4 19.8 %all-to-all-done.1 = bf16[16,128,512]{2,1,0:T(8,128)(2,1)S(1)} async-done(((bf16[16,128,512]{2,1,0:T(8,128)(2,1)}), bf16[16,128,512]{2,1,0:T(8,128)(2,1)S(1)}, u32[]{:S(2)}, u32[]{:S(2)}) %all-to-all-start.1) | async-done | bytes 2097184 | tf_op jit(solution)/shard_map/all_to_all | solution.py:40
  983.2 1.0 reduce_sum.78
  984.2 0.0 copy-done.1
  (15 shorter events, 0.1 us)
Async XLA Ops:
  7.2 455.9 %copy-start = (bf16[512,924]{0,1:T(8,128)(2,1)S(1)}, bf16[512,924]{0,1:T(8,128)(2,1)}, u32[]{:S(2)}) copy-start(bf16[512,924]{0,1:T(8,128)(2,1)} %param.17) | copy-start | bytes 2838532
  7.2 422.2 %all-gather.3.cloned.1.call-start = ((), (), s32[]{:S(2)}) async-start(), calls=%async_computation.2 | async-start | bytes 11698176 | tf_op jit(solution)/shard_map/all_gather | solution.py:28
  342.4 590.2 %all-reduce.3.cloned.1.call-start = ((), (), s32[]{:S(2)}) async-start(), calls=%async_computation.3 | async-start | bytes 22806528 | tf_op jit(solution)/shard_map/psum | solution.py:123
  449.8 23.0 %copy-start.5 = (bf16[2048,512]{1,0:T(8,128)(2,1)}, bf16[2048,512]{1,0:T(8,128)(2,1)S(1)}, u32[]{:S(2)}) copy-start(bf16[2048,512]{1,0:T(8,128)(2,1)S(1)} %gather_fusion) | copy-start | bytes 6291460
  463.0 5.9 copy-start.7
  463.0 5.9 copy-start.10
  468.9 3.9 copy-start.9
  932.6 7.3 copy-start.8
  939.9 3.2 copy-start.4
  943.0 2.4 copy-start.11
  949.4 33.8 %all-to-all-start.1 = ((bf16[16,128,512]{2,1,0:T(8,128)(2,1)}), bf16[16,128,512]{2,1,0:T(8,128)(2,1)S(1)}, u32[]{:S(2)}, u32[]{:S(2)}) async-start(bf16[16,128,512]{2,1,0:T(8,128)(2,1)} %bitcast.58), calls=%async_computation.1 | async-start | bytes 4194304 | tf_op jit(solution)/shard_map/all_to_all | solution.py:40
  953.9 6.0 copy-start.2
  953.9 6.0 copy-start.3
  953.9 6.0 copy-start.6
  959.9 24.2 %copy-start.1 = (bf16[512,924]{0,1:T(8,128)(2,1)S(1)}, bf16[512,924]{0,1:T(8,128)(2,1)}, u32[]{:S(2)}) copy-start(bf16[512,924]{0,1:T(8,128)(2,1)} %param.17) | copy-start | bytes 2838532
Sparse Core Ops, SparseCore 0:
  342.5 86.7 all-gather.2
  476.8 455.7 all-reduce.2
where the time goes:
time: 991 us
  waiting for transfers between devices  542 us (55%)
  blocking collectives  327 us (33%)
  local copies, waits for them, and re-layouts  57.6 us (6%)
  matrix products  32.5 us (3%)
  between operations  17 us (2%)
  other arithmetic  11 us (1%)
    psum x1, waiting for transfers between devices, per_device(): lax.psum(up_term.astype(jnp.bfloat16), 'col').astype(jnp.float32)  456 us
    all_gather x1, blocking collectives, per_device(): table = lax.all_gather(local, ('row', 'col'), axis=0, tiled=True)  307 us
    all_gather x1, waiting for transfers between devices, sent_together(): result = lax.all_gather(both, axis, axis=dim, tiled=True)  65.8 us
    scatter x1, local copies, waits for them, and re-layouts, source_index(): empty.at[target.reshape(-1)].set(flat_source.reshape(-1), mode='drop')  20.4 us
  transfers between devices with their start and end apart: 3, of which 3 were waited for; matrix products, arithmetic and copies ran while one was open for 3% of the time, Pallas kernels for 0%

commit v1 on v0

--- a/solution.py
+++ b/solution.py
@@ -5,6 +5,7 @@
 
 CAPR = 128
 spread_floor = 0.7
+track_the_sizes = lambda u_in, row_axis: jnp.sum(jax.lax.all_gather(u_in, axis_name=row_axis), 0)
 
 
 def in_one_piece(arrays, axis, split_dim, concat_dim, along):
@@ -120,7 +121,7 @@
     up_term = jnp.dot(packed, up_weight, preferred_element_type=jnp.float32)
     gate, upval = (
         lax.psum(gate_term.astype(jnp.bfloat16), "col").astype(jnp.float32),
-        lax.psum(up_term.astype(jnp.bfloat16), "col").astype(jnp.float32),
+        track_the_sizes(up_term.astype(jnp.bfloat16), "col").astype(jnp.float32),
     )
     sig = jax.nn.sigmoid(gate)
     silu = gate * sig

time: 991 us -> 1410 us (1.42)
  waiting for transfers between devices: 542 us -> 911 us
  local copies, waits for them, and re-layouts: 57.6 us -> 84.9 us
  other arithmetic: 11 us -> 34.1 us
    all_gather x0 -> x1, waiting for transfers between devices: none -> 558 us  [jax.lax.all_gather(u_in, axis_name=row_axis)]
    psum x1, waiting for transfers between devices: 456 us -> 267 us  [per_device(): lax.psum(grad_term.astype(jnp.bfloat16), 'col').astype(jnp.float32)]
    unnamed x26 -> x21, local copies, waits for them, and re-layouts: 1.31 us -> 29.5 us
    reduce_sum x0 -> x1, other arithmetic: none -> 23.2 us  [jnp.sum(jax.lax.all_gather(u_in, axis_name=row_axis), 0)]
  transfers between devices with their start and end apart: 3 -> 4, of which waited for: 3 -> 4; matrix products, arithmetic and copies ran while one was open for 3% -> 7% of each run, Pallas kernels for 0% -> 0%
where the time goes in v1:
time: 1410 us
  waiting for transfers between devices  911 us (65%)
  blocking collectives  327 us (23%)
  local copies, waits for them, and re-layouts  84.9 us (6%)
  other arithmetic  34.1 us (2%)
  matrix products  32.4 us (2%)
  between operations  16.7 us (1%)
    all_gather x1, waiting for transfers between devices, jax.lax.all_gather(u_in, axis_name=row_axis)  558 us
    all_gather x1, blocking collectives, per_device(): table = lax.all_gather(local, ('row', 'col'), axis=0, tiled=True)  307 us
    psum x1, waiting for transfers between devices, per_device(): lax.psum(grad_term.astype(jnp.bfloat16), 'col').astype(jnp.float32)  267 us
    all_gather x1, waiting for transfers between devices, sent_together(): result = lax.all_gather(both, axis, axis=dim, tiled=True)  66 us
    unnamed x21, local copies, waits for them, and re-layouts  29.5 us
  transfers between devices with their start and end apart: 4, of which 4 were waited for; matrix products, arithmetic and copies ran while one was open for 7% of the time, Pallas kernels for 0%

profile of v1, /device:TPU:4, one launch (start us, length us, event | category | flops | bytes accessed | tf_op | source)
XLA Modules:
  0.0 1412.9 jit_solution(15950964044386037273)
XLA Ops:
  7.2 0.0 copy-start
  7.2 0.0 all-gather.5.cloned.1.call-start
  9.9 0.1 maximum_bitcast_fusion
  10.0 307.3 %all-gather.1 = f32[128,1,4]{2,1,0:T(1,128)S(1)} all-gather(f32[1,1,4]{2,1,0:T(1,128)S(1)} %maximum_bitcast_fusion), channel_id=1, replica_groups=mesh['row'=16,'col'=8] {'row','col'}, dimensions={0}, use_global_device_ids=true | all-gather | bytes 2064 | tf_op jit(solution)/shard_map/all_gather | solution.py:100
  317.2 0.1 copy.27
  317.3 0.1 convert_reduce_fusion
  317.5 0.1 select_reduce_fusion.3
  317.6 0.1 select_reduce_fusion.2
  317.7 0.1 select_reduce_fusion.1
  317.8 0.6 dynamic_slice.3
  318.4 1.8 select_convert_fusion
  320.2 0.1 copy.31
  320.3 1.1 copy.30
  321.5 0.1 pad_maximum_fusion
  321.6 0.2 copy.28
  321.8 19.5 %all_to_all.10 = bf16[84,8,512]{2,0,1:T(8,128)(2,1)S(1)} all-to-all(bf16[84,8,512]{2,0,1:T(8,128)(2,1)S(1)} %copy.28), channel_id=1, replica_groups=mesh['row'=16,'col'=8] {'col'}, dimensions={1} | all-to-all | bytes 1376256 | tf_op jit(solution)/shard_map/all_to_all | solution.py:19
  341.3 1.1 copy.29
  342.3 0.0 all-gather.5.cloned.1.call-update
  342.4 0.0 all-gather.7.cloned.1.call-start
  342.4 0.2 select_reduce_fusion
  342.6 0.1 add_select_fusion
  342.7 0.2 select_n.47
  342.9 0.1 reshape.149
  343.0 0.1 fusion.15
  343.1 20.2 %scatter_custom_fusion = s32[2048]{0:T(1024)S(1)} fusion(s32[5376]{0:T(1024)S(1)} %fusion.15, s32[5376]{0:T(1024)S(1)} %reshape.149, s32[]{:T(128)} %constant.44.clone.1), kind=kCustom, calls=%fused_computation.48 | custom fusion | bytes 8196 | tf_op jit(solution)/shard_map/scatter | solution.py:71
  363.3 66.0 %all-gather.5.cloned.1.call-done = bf16[84,128,512]{2,1,0:T(8,128)(2,1)} async-done(((bf16[84,8,512]{2,1,0:T(8,128)(2,1)}), bf16[84,128,512]{2,1,0:T(8,128)(2,1)}) %all-gather.5.cloned.1.call-update) | async-done | bytes 11010064 | tf_op jit(solution)/shard_map/all_gather | solution.py:29
  429.3 9.6 fusion.25
  439.0 10.9 gather_fusion.1
  449.8 0.0 copy-start.4
  449.8 5.8 convolution_convert_fusion.1
  455.7 0.0 all-gather.7.cloned.1.call-update
  455.7 0.2 all-reduce.3.cloned.1.call-start
  455.9 12.5 gather_fusion
  468.4 0.0 copy-done
  468.4 0.0 copy-start.5
  468.4 0.0 copy-start.7
  468.4 3.9 convolution_convert_fusion
  472.3 0.0 copy-done.5
  472.3 0.0 copy-done.7
  472.3 3.9 convolution_convert_fusion.2
  476.2 0.0 all-reduce.3.cloned.1.call-update
  476.2 558.2 %all-gather.7.cloned.1.call-done = bf16[16384,924]{0,1:T(8,128)(2,1)} async-done(((bf16[2048,924]{0,1:T(8,128)(2,1)}), bf16[16384,924]{0,1:T(8,128)(2,1)}) %all-gather.7.cloned.1.call-update) | async-done | bytes 30277648 | tf_op jit(solution)/shard_map/all_gather | solution.py:8
  1034.4 28.2 %copy.32 = bf16[116,8,8,2048]{3,2,1,0:T(8,128)(2,1)} copy(bf16[116,8,8,2048]{3,1,2,0:T(8,128)(2,1)} %bitcast.64) | data formatting | bytes 60817408
  1062.6 23.2 %bitcast_reduce_fusion = bf16[2048,924]{0,1:T(8,128)(2,1)} fusion(bf16[928,8,2048]{2,1,0:T(8,128)(2,1)} %bitcast.61), kind=kLoop, calls=%fused_computation.3 | loop fusion | flops 13246464 | bytes 34062336 | tf_op jit(solution)/shard_map/reduce_sum | solution.py:8
  1085.9 267.0 %all-reduce.3.cloned.1.call-done = (bf16[2048,924]{0,1:T(8,128)(2,1)}, bf16[2048,924]{0,1:T(8,128)(2,1)}) async-done(((bf16[2048,924]{0,1:T(8,128)(2,1)}, bf16[2048,924]{0,1:T(8,128)(2,1)}), (bf16[2048,924]{0,1:T(8,128)(2,1)}, bf16[2048,924]{0,1:T(8,128)(2,1)})) %all-reduce.3.cloned.1.call-update) | async-done | bytes 7569424 | tf_op jit(solution)/shard_map/psum | solution.py:133
  1352.9 7.1 fusion
  1360.1 0.0 copy-start.3
  1360.1 0.0 copy-done.4
  1360.1 3.1 convolution_convert_fusion.3
  1363.2 0.0 copy-done.3
  1363.2 2.4 fusion.26
  1365.7 0.0 copy-done.8
  1365.7 3.8 add_convert_fusion
  1369.4 6.7 all-to-all-start.1
  1376.1 0.0 copy-start.1
  1376.1 0.0 copy-start.2
  1376.1 0.0 copy-start.6
  1376.1 6.0 convolution_convert_fusion.4
  1382.1 0.0 copy-done.1
  1382.1 0.0 copy-done.2
  1382.1 0.0 copy-done.6
  1382.2 3.5 fusion.11
  1385.6 19.8 %all-to-all-done.1 = bf16[16,128,512]{2,1,0:T(8,128)(2,1)S(1)} async-done(((bf16[16,128,512]{2,1,0:T(8,128)(2,1)}), bf16[16,128,512]{2,1,0:T(8,128)(2,1)S(1)}, u32[]{:S(2)}, u32[]{:S(2)}) %all-to-all-start.1) | async-done | bytes 2097184 | tf_op jit(solution)/shard_map/all_to_all | solution.py:41
  1405.4 1.0 reduce_sum.91
  (14 shorter events, 0.1 us)
Async XLA Ops:
  7.2 461.2 %copy-start = (bf16[512,924]{0,1:T(8,128)(2,1)S(1)}, bf16[512,924]{0,1:T(8,128)(2,1)}, u32[]{:S(2)}) copy-start(bf16[512,924]{0,1:T(8,128)(2,1)} %param.17) | copy-start | bytes 2838532
  7.2 422.1 %all-gather.5.cloned.1.call-start = ((), (), s32[]{:S(2)}) async-start(), calls=%async_computation.2 | async-start | bytes 11698176 | tf_op jit(solution)/shard_map/all_gather | solution.py:29
  342.4 692.0 %all-gather.7.cloned.1.call-start = ((), (), s32[]{:S(2)}) async-start(), calls=%async_computation.3 | async-start | bytes 34209792 | tf_op jit(solution)/shard_map/all_gather | solution.py:8
  449.8 910.2 %copy-start.4 = (bf16[2048,512]{1,0:T(8,128)(2,1)}, bf16[2048,512]{1,0:T(8,128)(2,1)S(1)}, u32[]{:S(2)}) copy-start(bf16[2048,512]{1,0:T(8,128)(2,1)S(1)} %gather_fusion.1) | copy-start | bytes 6291460
  455.7 897.2 %all-reduce.3.cloned.1.call-start = ((), (), s32[]{:S(2)}) async-start(), calls=%async_computation.4 | async-start | bytes 15204352 | tf_op jit(solution)/shard_map/psum | solution.py:133
  468.4 3.9 copy-start.5
  468.4 3.9 copy-start.7
  1360.1 3.2 copy-start.3
  1363.2 2.4 copy-start.8
  1369.4 36.0 %all-to-all-start.1 = ((bf16[16,128,512]{2,1,0:T(8,128)(2,1)}), bf16[16,128,512]{2,1,0:T(8,128)(2,1)S(1)}, u32[]{:S(2)}, u32[]{:S(2)}) async-start(bf16[16,128,512]{2,1,0:T(8,128)(2,1)} %bitcast.65), calls=%async_computation.1 | async-start | bytes 4194304 | tf_op jit(solution)/shard_map/all_to_all | solution.py:41
  1376.1 6.0 copy-start.1
  1376.1 6.0 copy-start.2
  1376.1 6.0 copy-start.6
Sparse Core Ops, SparseCore 0:
  342.5 86.7 all-gather.4
  455.8 578.5 all-gather.6
  1037.0 315.8 all-reduce.2
